TPU v7x, 256 devices: a whole 4x4x8 slice. The times are simulated.
256 devices in a mesh: tour: 16 (over z_hi, x), team: 16 (over y, z_lo, core).
Axes of the slice: x: 4, y: 4, z: 8 (z_hi: 4, z_lo: 2; z = z_hi * 2 + z_lo), core: 2. Of those that a mesh axis runs over, the one named last changes fastest.
Arguments:
- embeddings: float32 [65536, 128], P(('tour', 'team')), may hold values from -120 to 120
Outputs:
- embedding_grad: float32 [65536, 128], P(('tour', 'team'))
- uniformity_loss: float32 [], replicated
All inputs are finite; a program needn't handle non-finite values.
Results may differ from a plain program's by a relative error of at most 0.0012.
Values may be sent and summed in bfloat16 or wider, within the bound.
A program may use at most 128 MiB of HBM per device.

v0:
```python
import jax
import jax.numpy as jnp
from jax import lax
from jax.sharding import PartitionSpec as P


def tile_weights(row_block, col_part):
    scores = lax.dot_general(
        row_block, col_part, (((1,), (1,)), ((), ())), preferred_element_type=jnp.float32
    )
    return jnp.exp(4.0 * scores - 4.0)


def fold_piece(row_block, carried, piece):
    pull_sum, weight_sum = carried
    span_rows = min(piece.shape[0], 512)
    for offset in range(0, piece.shape[0], span_rows):
        col_part = piece[offset : offset + span_rows]
        weights = tile_weights(row_block, col_part)
        weight_sum = weight_sum + jnp.sum(weights)
        pull_sum = pull_sum + jnp.dot(
            weights.astype(jnp.bfloat16), col_part, preferred_element_type=jnp.float32
        )
    return (pull_sum, weight_sum)


def per_device(embeddings):
    squares = jnp.sum(embeddings * embeddings, axis=1, keepdims=True)
    inv_norm = lax.rsqrt(squares + 1e-06)
    direction = embeddings * inv_norm
    unit = direction.astype(jnp.bfloat16)
    unit_wide = unit.astype(jnp.float32)
    self_weight = jnp.exp(4.0 * jnp.sum(unit_wide * unit_wide, axis=1) - 4.0)
    width = unit.shape[1]
    row_block = lax.all_gather(unit, "team", axis=0, tiled=True)
    initial = (jnp.zeros((row_block.shape[0], width), jnp.float32), jnp.zeros((), jnp.float32))
    pull_rows, weight_sum = fold_piece(
        row_block, initial, lax.all_gather(unit, "tour", axis=0, tiled=True)
    )
    pull_sum = lax.psum_scatter(pull_rows, "team", scatter_dimension=0, tiled=True)
    pair_total = lax.psum(weight_sum - jnp.sum(self_weight), ("tour", "team"))
    total_rows = float(unit.shape[0] * lax.axis_size("tour") * lax.axis_size("team"))
    uniformity_loss = jnp.log(pair_total / (total_rows * (total_rows - 1.0)))
    pull_sum = pull_sum - self_weight[:, None] * unit_wide
    radial = jnp.sum(direction * pull_sum, axis=1, keepdims=True)
    factor = total_rows * total_rows / 8.0 / pair_total
    embedding_grad = factor * inv_norm * (pull_sum - direction * radial)
    return (embedding_grad, uniformity_loss)


def solution(mesh):
    placed = (P(("tour", "team"), None),)
    return jax.shard_map(
        per_device,
        mesh=mesh,
        in_specs=placed,
        out_specs=(P(("tour", "team"), None), P()),
        check_vma=False,
    )
```

profile of v0, /device:TPU:1, one launch (start us, length us, event | category | flops | bytes accessed | tf_op | source)
XLA Modules:
  0.0 254.1 jit_solution(16437439809809210894)
XLA Ops:
  7.2 0.0 all-gather.5.cloned.1.call-start
  7.2 1.0 multiply_reduce_fusion.1
  8.2 1.6 fusion.41
  9.9 0.0 all-gather.5.cloned.1.call-update
  9.9 0.0 all-gather.3.cloned.1.call-start
  10.0 0.7 all-gather.3.cloned.1.call-update
  10.7 0.0 reduce-scatter.2.cloned.1.call-start
  10.7 56.4 %all-gather.5.cloned.1.call-done = bf16[4096,128]{1,0:T(8,128)(2,1)} async-done(((bf16[256,128]{1,0:T(8,128)(2,1)}), bf16[4096,128]{1,0:T(8,128)(2,1)}) %all-gather.5.cloned.1.call-update) | async-done | bytes 1048592 | tf_op jit(solution)/shard_map/all_gather | solution.py:38
  67.1 0.0 copy-start.1
  67.1 36.4 %all-gather.3.cloned.1.call-done = bf16[4096,128]{1,0:T(8,128)(2,1)} async-done(((bf16[256,128]{1,0:T(8,128)(2,1)}), bf16[4096,128]{1,0:T(8,128)(2,1)}) %all-gather.3.cloned.1.call-update) | async-done | bytes 1048592 | tf_op jit(solution)/shard_map/all_gather | solution.py:35
  103.5 0.0 copy-start
  103.5 4.3 %fusion.1 = (f32[]{:T(128)}, f32[4096,512]{1,0:T(8,128)S(1)}) fusion(bf16[4096,128]{1,0:T(8,128)(2,1)} %all-gather.3.cloned.1.call-done, bf16[4096,128]{1,0:T(8,128)(2,1)} %all-gather.5.cloned.1.call-done), kind=kOutput, calls=%fused_computation.9 | convolution fusion | flops 543162368 | bytes 9568260 | tf_op jit(solution)/shard_map/dot_general | solution.py:8
  107.8 0.0 copy-done.1
  107.8 0.0 copy-done
  107.8 2.9 %fusion.3 = (f32[]{:T(128)}, f32[4096,512]{1,0:T(8,128)S(1)}) fusion(bf16[4096,128]{1,0:T(8,128)(2,1)S(1)} %copy-done, bf16[4096,128]{1,0:T(8,128)(2,1)S(1)} %copy-done.1), kind=kOutput, calls=%fused_computation.11 | convolution fusion | flops 543162368 | bytes 9568260 | tf_op jit(solution)/shard_map/dot_general | solution.py:8
  110.7 3.0 %fusion.5 = (f32[]{:T(128)}, f32[4096,512]{1,0:T(8,128)S(1)}) fusion(bf16[4096,128]{1,0:T(8,128)(2,1)S(1)} %copy-done, bf16[4096,128]{1,0:T(8,128)(2,1)S(1)} %copy-done.1), kind=kOutput, calls=%fused_computation.13 | convolution fusion | flops 543162368 | bytes 9568260 | tf_op jit(solution)/shard_map/dot_general | solution.py:8
  113.7 6.1 %fusion.7 = (f32[]{:T(128)}, f32[4096,512]{1,0:T(8,128)}) fusion(bf16[4096,128]{1,0:T(8,128)(2,1)S(1)} %copy-done, bf16[4096,128]{1,0:T(8,128)(2,1)S(1)} %copy-done.1), kind=kOutput, calls=%fused_computation.15 | convolution fusion | flops 543162368 | bytes 9568260 | tf_op jit(solution)/shard_map/dot_general | solution.py:8
  119.8 6.1 %fusion.9 = (f32[]{:T(128)}, f32[4096,512]{1,0:T(8,128)}) fusion(bf16[4096,128]{1,0:T(8,128)(2,1)S(1)} %copy-done, bf16[4096,128]{1,0:T(8,128)(2,1)S(1)} %copy-done.1), kind=kOutput, calls=%fused_computation.17 | convolution fusion | flops 543162368 | bytes 9568260 | tf_op jit(solution)/shard_map/dot_general | solution.py:8
  125.9 6.3 %fusion.11 = (f32[]{:T(128)}, f32[4096,512]{1,0:T(8,128)}) fusion(bf16[4096,128]{1,0:T(8,128)(2,1)S(1)} %copy-done, bf16[4096,128]{1,0:T(8,128)(2,1)S(1)} %copy-done.1), kind=kOutput, calls=%fused_computation.19 | convolution fusion | flops 543162368 | bytes 9568260 | tf_op jit(solution)/shard_map/dot_general | solution.py:8
  132.3 6.1 %fusion.13 = (f32[]{:T(128)}, f32[4096,512]{1,0:T(8,128)}) fusion(bf16[4096,128]{1,0:T(8,128)(2,1)S(1)} %copy-done, bf16[4096,128]{1,0:T(8,128)(2,1)S(1)} %copy-done.1), kind=kOutput, calls=%fused_computation.21 | convolution fusion | flops 543162368 | bytes 9568260 | tf_op jit(solution)/shard_map/dot_general | solution.py:8
  138.3 3.0 %fusion.15 = (f32[]{:T(128)}, f32[4096,512]{1,0:T(8,128)S(1)}) fusion(bf16[4096,128]{1,0:T(8,128)(2,1)S(1)} %copy-done, bf16[4096,128]{1,0:T(8,128)(2,1)S(1)} %copy-done.1), kind=kOutput, calls=%fused_computation.23 | convolution fusion | flops 543162368 | bytes 9568260 | tf_op jit(solution)/shard_map/dot_general | solution.py:8
  141.3 1.5 fusion.23
  142.7 0.0 slice-start
  142.7 1.5 convolution_add_fusion.6
  144.3 0.0 slice-start.1
  144.3 0.0 slice-start.2
  144.3 1.5 convolution_add_fusion.5
  145.8 0.0 slice-done
  145.8 0.8 slice-done.1
  146.6 1.7 convolution_add_fusion.4
  148.4 0.0 slice-done.2
  148.4 0.7 slice-done.3
  149.1 1.5 convolution_add_fusion.3
  150.6 0.0 slice-done.4
  150.6 0.9 slice-done.5
  151.5 1.5 convolution_add_fusion.2
  153.0 0.0 slice-done.6
  153.1 0.9 slice-done.7
  154.0 1.5 convolution_add_fusion.1
  155.5 0.0 copy-start.2
  155.5 2.9 %convolution_add_fusion = f32[4096,128]{1,0:T(8,128)} fusion(f32[4096,128]{1,0:T(8,128)S(1)} %convolution_add_fusion.1, f32[4096,512]{1,0:T(8,128)S(1)} %get-tuple-element.21, bf16[4096,128]{1,0:T(8,128)(2,1)S(1)} %copy-done.1), kind=kOutput, calls=%fused_computation.24 | convolution fusion | flops 543686656 | bytes 12713984 | tf_op jit(solution)/shard_map/dot_general | solution.py:21
  158.4 0.0 reduce-scatter.2.cloned.1.call-update
  158.4 0.7 fusion.83
  164.8 77.3 %psum.7 = f32[]{:T(128)} all-reduce(f32[]{:T(128)S(6)} %sub.45), channel_id=1, replica_groups=mesh['tour'=16,'team'=16] {'tour','team'}, use_global_device_ids=true, to_apply=%region_11.0 | all-reduce | flops 1 | bytes 8 | tf_op jit(solution)/shard_map/psum | solution.py:41
  243.5 0.0 reduce-scatter.2.cloned.1.call-done
  243.5 0.0 copy-done.2
  243.5 1.1 multiply_reduce_fusion
  244.7 1.8 subtract_multiply_fusion
  (11 shorter events, 0.0 us)
Async XLA Ops:
  7.2 59.9 %all-gather.5.cloned.1.call-start = ((), (), s32[]{:S(2)}) async-start(), calls=%async_computation.2 | async-start | bytes 1114112 | tf_op jit(solution)/shard_map/all_gather | solution.py:38
  9.9 93.6 %all-gather.3.cloned.1.call-start = ((), (), s32[]{:S(2)}) async-start(), calls=%async_computation.1 | async-start | bytes 1114112 | tf_op jit(solution)/shard_map/all_gather | solution.py:35
  10.7 232.9 %reduce-scatter.2.cloned.1.call-start = ((), (), s32[]{:S(2)}) async-start(), calls=%async_computation.3 | async-start | bytes 2228224 | tf_op jit(solution)/shard_map/reduce_scatter | solution.py:40
  67.1 40.7 %copy-start.1 = (bf16[4096,128]{1,0:T(8,128)(2,1)S(1)}, bf16[4096,128]{1,0:T(8,128)(2,1)}, u32[]{:S(2)}) copy-start(bf16[4096,128]{1,0:T(8,128)(2,1)} %all-gather.5.cloned.1.call-done) | copy-start | bytes 3145732
  103.5 4.3 %copy-start = (bf16[4096,128]{1,0:T(8,128)(2,1)S(1)}, bf16[4096,128]{1,0:T(8,128)(2,1)}, u32[]{:S(2)}) copy-start(bf16[4096,128]{1,0:T(8,128)(2,1)} %all-gather.3.cloned.1.call-done) | copy-start | bytes 3145732
  142.7 3.1 %slice-start = ((s8[8388608]{0:T(1024)(128)(4,1)}), s8[4194304]{0:T(1024)(128)(4,1)S(1)}, s32[]{:S(2)}) async-start(s8[8388608]{0:T(1024)(128)(4,1)} %bitcast.8), calls=%async_computation.4 | async-start | bytes 8388608
  144.3 2.4 slice-start.1
  144.3 4.1 %slice-start.2 = ((s8[8388608]{0:T(1024)(128)(4,1)}), s8[4194304]{0:T(1024)(128)(4,1)S(1)}, s32[]{:S(2)}) async-start(s8[8388608]{0:T(1024)(128)(4,1)} %bitcast.10), calls=%async_computation.6 | async-start | bytes 8388608
  146.6 2.5 slice-start.3
  146.6 4.0 %slice-start.4 = ((s8[8388608]{0:T(1024)(128)(4,1)}), s8[4194304]{0:T(1024)(128)(4,1)S(1)}, s32[]{:S(2)}) async-start(s8[8388608]{0:T(1024)(128)(4,1)} %bitcast.12), calls=%async_computation.8 | async-start | bytes 8388608
  149.1 2.4 slice-start.5
  149.1 4.0 %slice-start.6 = ((s8[8388608]{0:T(1024)(128)(4,1)}), s8[4194304]{0:T(1024)(128)(4,1)S(1)}, s32[]{:S(2)}) async-start(s8[8388608]{0:T(1024)(128)(4,1)} %bitcast.14), calls=%async_computation.10 | async-start | bytes 8388608
  151.5 2.4 slice-start.7
  155.5 88.0 %copy-start.2 = (f32[256,128]{1,0:T(8,128)S(1)}, f32[256,128]{1,0:T(8,128)}, u32[]{:S(2)}) copy-start(f32[256,128]{1,0:T(8,128)} %param.1) | copy-start | bytes 393220
Sparse Core Ops, SparseCore 0:
  11.0 56.0 all-gather.4
  69.5 33.9 all-gather.2
  158.5 63.8 reduce-scatter.1
where the time goes:
time: 254 us
  waiting for transfers between devices  93.5 us (37%)
  blocking collectives  77.3 us (30%)
  matrix products  51.4 us (20%)
  between operations  22.2 us (9%)
  other arithmetic  6.23 us (2%)
  local copies, waits for them, and re-layouts  3.36 us (1%)
    psum x1, blocking collectives, per_device(): pair_total = lax.psum(weight_sum - jnp.sum(self_weight), ('tour', 'team'))  77.3 us
    all_gather x1, waiting for transfers between devices, per_device(): lax.all_gather(unit, 'tour', axis=0, tiled=True)  56.4 us
    dot_general x8, matrix products, tile_weights(): lax.dot_general(row_block, col_part, (((1,), (1,)), ((), ())), preferred_...  37.8 us
    all_gather x1, waiting for transfers between devices, per_device(): row_block = lax.all_gather(unit, 'team', axis=0, tiled=True)  36.4 us
    dot_general x8, matrix products, fold_piece(): jnp.dot(weights.astype(jnp.bfloat16), col_part, preferred_element_type=jn...  13.6 us
  transfers between devices with their start and end apart: 3, of which 2 were waited for; matrix products, arithmetic and copies ran while one was open for 0% of the time, Pallas kernels for 0%

commit v1 on v0

v1 whole, which is shorter than its diff:
```python
import math

import jax
import jax.numpy as jnp
from jax import lax
from jax.experimental import pallas as pl
from jax.experimental.pallas import tpu as pltpu
from jax.sharding import PartitionSpec as P

F32, BF16 = jnp.float32, jnp.bfloat16
MESH = pl.DeviceIdType.MESH
SCALE = 4.0 / math.log(2.0)
SHIFT = math.exp(-4.0)
NX, NY, NZ = 4, 4, 8
D, B = 128, 256
H = B // 2
SPAN = 200.0
MSG = D + 16
LO, HI = pl.ds(0, H), pl.ds(H, H)

OFFSETS = (0, 1, 2, 3, 4, -1, -2, -3)
SLOT = {o: p for p, o in enumerate(OFFSETS)}
CHIPS = ((0, 0), (1, 0), (3, 0), (0, 1), (0, 3), (2, 0), (0, 2), (1, 1), (1, 3), (3, 1), (3, 3),
         (1, 2), (3, 2), (2, 1), (2, 3), (2, 2))
PLACE = {chip: k for k, chip in enumerate(CHIPS)}
GROUPS = ((0, 0, 5), (1, 0, 5), (0, 5, 7), (1, 5, 7), (0, 7, 11), (1, 7, 11), (0, 11, 16), (1, 11, 16))
GROUP_AT = (3.1, 4.4, 4.9, 6.0, 6.3, 7.4, 8.8, 9.9)
ROW_AT = {0: 0.0, 1: 3.0, -1: 3.0, 2: 6.1, -2: 6.1, 3: 9.2, -3: 9.2, 4: 10.2}
SCORE_US, PULL_US = 0.037, 0.018


def plan():
    events = [("rows1", 3.0), ("cols1", 3.1), ("sib1", 4.4), ("cols2", 4.9), ("rows2", 6.0), ("sib2", 6.0),
              ("cols3", 6.3), ("sib3", 7.4), ("cols4", 8.8), ("rows3", 9.2), ("sib4", 9.9), ("rows4", 10.2)]
    n = len(GROUPS)
    goals = [("S", o, g) for g in range(n) for o in (0, 1, 2, 3, 4)]
    goals += [("P", 4, g) for g in range(n)]
    for o in (3, 2, 1):
        goals += [("S", -o, g) for g in range(n)]
        goals += [("P", s * o, g) for s in (-1, 1) for g in range(n)]
    goals += [("P", 0, g) for g in range(n)]
    out, done, now = [], set(), 0.0
    todo = list(goals)

    def finish(kind, offsets):
        return all((kind, o, g) in done for o in offsets for g in range(n))

    after = [("total", lambda: finish("S", (0, 1, 2, 3, 4)))]
    after += [("send4", lambda: finish("P", (4,)))]
    after += [("send3", lambda: finish("P", (3,))), ("send-3", lambda: finish("P", (-3,)))]
    after += [("send1", lambda: finish("P", (1,))), ("send-1", lambda: finish("P", (-1,)))]
    ready2 = lambda o: finish("P", (o,)) and now >= sent.get("send3", 1e9) + 3.8
    after += [("send2", lambda: ready2(2)), ("send-2", lambda: ready2(-2))]
    sent = {}
    while todo or events or after:
        while events and events[0][1] <= now:
            out.append((events.pop(0)[0],))
        for item in list(after):
            if item[1]():
                out.append((item[0],))
                sent[item[0]] = now
                after.remove(item)
                if item[0] == "total":
                    events.append(("plane", now + 5.5))
        pick = None
        for task in todo:
            kind, o, g = task
            if kind == "S":
                if max(GROUP_AT[g], ROW_AT[o]) <= now:
                    pick = task
                    break
            elif ("S", o, g) in done:
                pick = task
                break
        if pick is None:
            now += 0.05
            continue
        todo.remove(pick)
        done.add(pick)
        out.append(pick)
        core, a, b = GROUPS[pick[2]]
        now += (b - a) * (SCORE_US if pick[0] == "S" else PULL_US)
    return out


def dot(a, b):
    return lax.dot_general(a, b, (((1,), (0,)), ((), ())), preferred_element_type=F32)


def encode(x, msg, cols):
    top = (jnp.max(jnp.abs(x), axis=0, keepdims=True) * 1.01 + 1e-30).astype(BF16)
    y = jnp.exp2(jnp.abs(x) * (SPAN / top.astype(F32)) - SPAN / 2)
    msg[0:D, cols] = jnp.where(x < 0, -y, y).astype(BF16)
    msg[D:MSG, cols] = jnp.broadcast_to(top, (MSG - D, x.shape[1]))


def decode(msg, cols):
    y = msg[0:D, cols].astype(F32)
    top = msg[D:MSG, cols].astype(F32)[0:1]
    x = (jnp.log(jnp.abs(y)) * (1.0 / math.log(2.0)) + SPAN / 2) * (top * (1.0 / SPAN))
    return jnp.where(y < 0, -x, x)


class Net:
    def __init__(self, send, recv):
        t, m = lax.axis_index("tour"), lax.axis_index("team")
        self.z = (t // 4) * 2 + (m // 2) % 2
        self.x, self.y, self.c = t % 4, m // 4, m % 2
        self.send, self.recv = send, recv
        self.copies = []

    def at(self, dx=0, dy=0, dz=0, dc=0):
        x, y = (self.x + dx) % NX, (self.y + dy) % NY
        z, c = (self.z + dz) % NZ, (self.c + dc) % 2
        return ((z // 2) * 4 + x, (y * 2 + z % 2) * 2 + c)

    def copy(self, src, dst, **where):
        i = len(self.copies)
        self.copies.append(pltpu.make_async_remote_copy(
            src_ref=src, dst_ref=dst, send_sem=self.send.at[i], recv_sem=self.recv.at[i],
            device_id=self.at(**where), device_id_type=MESH))
        return self.copies[-1]


COPIES = 8 + 6 + 18 + 5 + 8 + 30


def kernel(emb_ref, out_ref, tot_ref, cols, colt, rowt, acc, w, once, twice, mo, mi, sums, send, recv):
    net = Net(send, recv)
    line = [(dz, dc) for dz in range(NZ) for dc in range(2) if (dz, dc) != (0, 0)]
    plane = [(dx, dy) for dx in range(NX) for dy in range(NY) if (dx, dy) != (0, 0)]

    barrier = pltpu.get_barrier_semaphore()
    for dz, dc in line:
        pl.semaphore_signal(barrier, inc=1, device_id=net.at(dz=dz, dc=dc), device_id_type=MESH)
    for dx, dy in plane:
        pl.semaphore_signal(barrier, inc=1, device_id=net.at(dx=dx, dy=dy), device_id_type=MESH)

    row = lambda o: rowt.at[SLOT[o]]
    rows1 = [net.copy(row(0), row(-1), dz=1), net.copy(row(0), row(1), dz=-1)]
    rows2 = [net.copy(row(-1), row(-2), dz=1), net.copy(row(1), row(2), dz=-1)]
    rows3 = [net.copy(row(-2), row(-3), dz=1), net.copy(row(2), row(3), dz=-1)]
    rows4 = [net.copy(rowt.at[SLOT[-2], :, LO], rowt.at[SLOT[4], :, LO], dz=2),
             net.copy(rowt.at[SLOT[2], :, HI], rowt.at[SLOT[4], :, HI], dz=-2)]
    place = lambda dx, dy: PLACE[dx % NX, dy % NY]
    direct = {(dx, dy): net.copy(cols.at[0, 0], cols.at[0, place(-dx, -dy)], dx=dx, dy=dy)
              for dx, dy in ((1, 0), (3, 0), (0, 1), (0, 3), (2, 0), (0, 2))}
    by_y = {(a, b): net.copy(cols.at[0, place(a, 0), LO], cols.at[0, place(a, -b), LO], dy=b)
            for b in (1, 3, 2) for a in (1, 3, 2)}
    by_x = {(a, b): net.copy(cols.at[0, place(0, a), HI], cols.at[0, place(-b, a), HI], dx=b)
            for b in (1, 3, 2) for a in (1, 3, 2)}
    sib = [net.copy(cols.at[0, pl.ds(a, b - a)], cols.at[1, pl.ds(a, b - a)], dc=1)
           for a, b in ((0, 1), (1, 5), (5, 7), (7, 11), (11, 16))]
    far = [net.copy(mo.at[SLOT[4], :, LO], mi.at[0, :, LO], dz=2), net.copy(mo.at[SLOT[4], :, HI], mi.at[1, :, HI], dz=-2)]
    third = {3: net.copy(mo.at[SLOT[3]], mi.at[2], dz=1), -3: net.copy(mo.at[SLOT[-3]], mi.at[3], dz=-1)}
    second = {2: net.copy(mo.at[SLOT[2]], mi.at[4], dz=2), -2: net.copy(mo.at[SLOT[-2]], mi.at[5], dz=-2)}
    first = {1: net.copy(mo.at[SLOT[1]], mi.at[6], dz=1), -1: net.copy(mo.at[SLOT[-1]], mi.at[7], dz=-1)}
    tell_line = [net.copy(sums.at[0], sums.at[1 + i], dz=dz, dc=dc) for i, (dz, dc) in enumerate(line)]
    tell_plane = [net.copy(sums.at[16], sums.at[17 + i], dx=dx, dy=dy) for i, (dx, dy) in enumerate(plane)]

    emb = emb_ref[...]
    inv_norm = lax.rsqrt(jnp.sum(emb * emb, axis=1, keepdims=True) + 1e-06)
    direction = emb * inv_norm
    own = direction.astype(BF16)
    wide = own.astype(F32)
    cols[0, 0] = own
    rowt[0] = wide.T.astype(BF16)
    self_weight = jnp.exp(4.0 * jnp.sum(wide * wide, axis=1, keepdims=True) - 4.0)
    once[...] = jnp.zeros_like(once)
    twice[...] = jnp.zeros_like(twice)
    pl.semaphore_wait(barrier, len(line) + len(plane))

    for c in rows1 + list(direct.values()) + [sib[0]]:
        c.start()

    turned, begun = set(), set()

    def scores(o, g):
        core, a, b = GROUPS[g]
        n = (b - a) * B
        r = (core * 16 + a) * B
        e = jnp.exp2(dot(cols[core, a:b].reshape(n, D), rowt[SLOT[o]]) * SCALE)
        if o >= 0:
            total = once if o in (0, 4) else twice
            total[...] += jnp.sum(e.reshape(n // 64, 64, B), axis=0)
        w[SLOT[o], r:r + n] = e.astype(BF16)

    def pull(o, g):
        core, a, b = GROUPS[g]
        n = (b - a) * B
        r = (core * 16 + a) * B
        if g not in turned:
            turned.add(g)
            for k in range(a, b):
                s = (core * 16 + k) * B
                colt[:, s:s + B] = cols[core, k].astype(F32).T.astype(BF16)
        p = dot(colt[:, r:r + n], w[SLOT[o], r:r + n])
        if o in begun:
            acc[SLOT[o]] += p
        else:
            begun.add(o)
            acc[SLOT[o]] = p

    def wait(copies):
        for c in copies:
            c.wait_recv()

    def start(copies):
        for c in copies:
            c.start()

    near, both = (1, 3), (1, 3, 2)

    def event(name):
        if name == "rows1":
            wait(rows1)
            start(rows2)
        elif name == "rows2":
            wait(rows2)
            start(rows3 + rows4)
        elif name == "rows3":
            wait(rows3)
        elif name == "rows4":
            wait(rows4)
        elif name == "cols1":
            wait([direct[1, 0], direct[3, 0], direct[0, 1], direct[0, 3]])
            start([f[a, b] for b in both for a in near for f in (by_y, by_x)])
            start([sib[1]])
        elif name == "cols2":
            wait([direct[2, 0], direct[0, 2]])
            start([f[2, b] for b in both for f in (by_y, by_x)])
            start([sib[2]])
        elif name == "cols3":
            wait([f[a, b] for b in near for a in near for f in (by_y, by_x)])
            start([sib[3]])
        elif name == "cols4":
            wait([f[a, b] for b in both for a in both for f in (by_y, by_x) if 2 in (a, b)])
            start([sib[4]])
        elif name == "sib1":
            wait(sib[0:2])
        elif name.startswith("sib"):
            wait([sib[int(name[3:])]])
        elif name == "total":
            local = (2.0 * jnp.sum(twice[...]) + jnp.sum(once[...])) * SHIFT - jnp.sum(self_weight)
            sums[0] = jnp.full((8, 128), local, F32)
            start(tell_line)
        elif name == "plane":
            wait(tell_line)
            total = sums[0]
            for i in range(len(line)):
                total = total + sums[1 + i]
            sums[16] = total
            start(tell_plane)
        else:
            o = int(name[4:])
            p = SLOT[o]
            if abs(o) == 2:
                half, i = (LO, 0) if o > 0 else (HI, 1)
                wait([far[i], third[3 if o > 0 else -3]])
                acc[p, :, half] += decode(mi.at[i], half)
                encode(acc[p] + decode(mi.at[2 + i], slice(None)), mo.at[p], slice(None))
                start([second[o]])
            else:
                encode(acc[p], mo.at[p], slice(None))
                start({4: far, 3: [third[3]], -3: [third[-3]], 1: [first[1]], -1: [first[-1]]}[o])

    for task in plan():
        if task[0] == "S":
            scores(*task[1:])
        elif task[0] == "P":
            pull(*task[1:])
        else:
            event(task[0])

    pulled = acc[0]
    for i, c in ((6, first[1]), (7, first[-1]), (4, second[2]), (5, second[-2])):
        c.wait_recv()
        pulled = pulled + decode(mi.at[i], slice(None))
    pulled = pulled.T * SHIFT - self_weight * wide
    radial = jnp.sum(direction * pulled, axis=1, keepdims=True)
    out_ref[...] = inv_norm * (pulled - direction * radial)
    wait(tell_plane)
    total = sums[16]
    for i in range(len(plane)):
        total = total + sums[17 + i]
    tot_ref[...] = total
    for c in net.copies:
        c.wait_send()


def per_device(embeddings):
    whole = pl.BlockSpec(memory_space=pltpu.VMEM)
    raw, total = pl.pallas_call(
        kernel,
        out_shape=(jax.ShapeDtypeStruct((B, D), F32), jax.ShapeDtypeStruct((8, 128), F32)),
        in_specs=[whole],
        out_specs=(whole, whole),
        scratch_shapes=[
            pltpu.VMEM((2, 16, B, D), BF16),
            pltpu.VMEM((D, 32 * B), BF16),
            pltpu.VMEM((8, D, B), BF16),
            pltpu.VMEM((8, D, B), F32),
            pltpu.VMEM((8, 32 * B, B), BF16),
            pltpu.VMEM((64, B), F32),
            pltpu.VMEM((64, B), F32),
            pltpu.VMEM((8, MSG, B), BF16),
            pltpu.VMEM((8, MSG, B), BF16),
            pltpu.VMEM((32, 8, 128), F32),
            pltpu.SemaphoreType.DMA((COPIES,)),
            pltpu.SemaphoreType.DMA((COPIES,)),
        ],
        compiler_params=pltpu.CompilerParams(
            collective_id=0, has_side_effects=True, vmem_limit_bytes=56 * 2**20),
        name="uniformity",
    )(embeddings)
    pair_total = total[0, 0]
    rows = float(B * lax.axis_size("tour") * lax.axis_size("team"))
    loss = jnp.log(pair_total / (rows * (rows - 1.0)))
    return raw * (rows * rows / 8.0 / pair_total), loss


def solution(mesh):
    return jax.shard_map(
        per_device,
        mesh=mesh,
        in_specs=(P(("tour", "team"), None),),
        out_specs=(P(("tour", "team"), None), P()),
        check_vma=False,
    )
```

time: 254 us -> 50.9 us (0.20)
  waiting for transfers between devices: 93.5 us -> 0 us
  blocking collectives: 77.3 us -> 0 us
  matrix products: 51.4 us -> 0 us
  Pallas kernels: 0 us -> 44.9 us
  between operations: 22.2 us -> 3.14 us
  other arithmetic: 6.23 us -> 1.57 us
    all_gather x2 -> x0, waiting for transfers between devices: 92.8 us -> none  [the longest x1 56.4 us: per_device(): lax.all_gather(unit, 'tour', axis=0, tiled=True)]
    psum x1 -> x0, blocking collectives: 77.3 us -> none  [per_device(): pair_total = lax.psum(weight_sum - jnp.sum(self_weight), ('tour', 'team'))]
    dot_general x16 -> x0, matrix products: 51.4 us -> none  [the longest x8 37.8 us: tile_weights(): lax.dot_general(row_block, col_part, (((1,), (1,)), ((), ())), preferred_...]
    pallas_call x0 -> x1, Pallas kernels: none -> 44.9 us  [per_device(): pl.pallas_call(kernel, out_shape=(jax.ShapeDtypeStruct((B, D), F32), jax....]
    reduce_sum x4 -> x0, other arithmetic: 4.45 us -> none  [the longest x1 1.64 us: per_device(): self_weight = jnp.exp(4.0 * jnp.sum(unit_wide * unit_wide, axis=1) - 4.0)]
    unnamed x22 -> x0, local copies, waits for them, and re-layouts: 3.36 us -> none
  transfers between devices with their start and end apart: 3 -> 0, of which waited for: 2 -> 0; matrix products, arithmetic and copies ran while one was open for 0% -> 0% of each run, Pallas kernels for 0% -> 0%
where the time goes in v1:
time: 50.9 us; the launch traced here: 50.8 us
  Pallas kernels  44.9 us (88%)
  between operations  3.14 us (6%)
  other arithmetic  1.57 us (3%)
  local copies, waits for them, and re-layouts  1.2 us (2%)
    pallas_call x1, Pallas kernels, per_device(): pl.pallas_call(kernel, out_shape=(jax.ShapeDtypeStruct((B, D), F32), jax....  44.9 us
    mul x1, other arithmetic, per_device(): return (raw * (rows * rows / 8.0 / pair_total), loss)  1.57 us
    slice x1, local copies, waits for them, and re-layouts, per_device(): pair_total = total[0, 0]  1.2 us

profile of v1, /device:TPU:1, one launch (start us, length us, event | category | flops | bytes accessed | tf_op | source)
XLA Modules:
  0.0 50.8 jit_solution(13472791196680490027)
XLA Ops:
  0.6 44.9 %uniformity.1 = (f32[256,128]{1,0:T(8,128)}, f32[8,128]{1,0:T(8,128)}) custom-call(f32[256,128]{1,0:T(8,128)} %emb_ref.1), custom_call_target="tpu_custom_call" | custom-call | tf_op jit(solution)/shard_map/uniformity/pallas_call | solution.py:293
  45.5 1.2 %slice.3 = f32[1,1]{1,0:T(1,128)} slice(f32[8,128]{1,0:T(8,128)} %get-tuple-element.5), slice={[0:1], [0:1]} | slice | bytes 8 | tf_op jit(solution)/shard_map/slice | solution.py:316
  48.1 1.6 %broadcast_multiply_fusion = f32[256,128]{1,0:T(8,128)} fusion(f32[256,128]{1,0:T(8,128)} %get-tuple-element.4, f32[]{:T(128)} %bitcast), kind=kLoop, calls=%fused_computation | loop fusion | flops 32768 | bytes 262148 | tf_op jit(solution)/shard_map/mul | solution.py:319

commit v2 on v1

v2 whole, which is shorter than its diff:
```python
import math

import jax
import jax.numpy as jnp
from jax import lax
from jax.experimental import pallas as pl
from jax.experimental.pallas import tpu as pltpu
from jax.sharding import PartitionSpec as P

F32, BF16 = jnp.float32, jnp.bfloat16
MESH = pl.DeviceIdType.MESH
SCALE = 4.0 / math.log(2.0)
SHIFT = math.exp(-4.0)
NX, NY, NZ = 4, 4, 8
D, B = 128, 256
H = B // 2
SPAN = 200.0
MSG = D + 16
LO, HI, ALL = pl.ds(0, H), pl.ds(H, H), pl.ds(0, B)

OFFSETS = (0, 1, -1, 2, -2, 3, -3, 4)
SLOT = {o: p for p, o in enumerate(OFFSETS)}
CHIPS = ((0, 0), (1, 0), (3, 0), (0, 1), (0, 3), (2, 0), (0, 2), (1, 1), (1, 3), (3, 1), (3, 3),
         (1, 2), (3, 2), (2, 1), (2, 3), (2, 2))
PLACE = {chip: k for k, chip in enumerate(CHIPS)}
GROUPS = ((0, 0, 5), (1, 0, 5), (0, 5, 7), (1, 5, 7), (0, 7, 11), (1, 7, 11), (0, 11, 15), (1, 11, 15), (0, 15, 16),
          (1, 15, 16))
EVENTS = (("rows1", 3.1), ("cols1", 3.2), ("sib1", 4.9), ("cols2", 5.4), ("sib2", 6.9), ("rows2", 7.5), ("cols3", 7.6),
          ("rows4", 8.4), ("sib3", 9.1), ("cols4", 9.2), ("cols5", 10.2), ("rows3", 10.5), ("sib4", 10.8), ("sib5", 11.7))
AT = dict(EVENTS)
GROUP_AT = tuple(AT[e] for e in ("cols1", "sib1", "cols2", "sib2", "cols3", "sib3", "cols4", "sib4",
                                "cols5", "sib5"))
ROW_AT = {0: 0.0, 1: AT["rows1"], -1: AT["rows1"], 2: AT["rows2"], -2: AT["rows2"], 3: AT["rows3"], -3: AT["rows3"],
          4: AT["rows4"]}
SCORE_US, PULL_US = 0.041, 0.020


def plan():
    events = list(EVENTS)
    n = len(GROUPS)
    goals = [("S", o, g) for g in range(n) for o in (0, 1, 2, 3, 4)]
    goals += [("S", -3, g) for g in range(n)]
    goals += [("P", o, g) for o in (4, 3, -3) for g in range(n)]
    for o in (2, 1):
        goals += [("S", -o, g) for g in range(n)]
        goals += [("P", s * o, g) for s in (-1, 1) for g in range(n)]
    goals += [("P", 0, g) for g in range(n)]
    out, done, now = [], set(), 0.0
    todo = list(goals)

    def finish(kind, offsets):
        return all((kind, o, g) in done for o in offsets for g in range(n))

    after = [("total", lambda: finish("S", (0, 1, 2, 3, 4)))]
    after += [("send4", lambda: finish("P", (4,)))]
    after += [("send3", lambda: finish("P", (3,))), ("send-3", lambda: finish("P", (-3,)))]
    after += [("send1", lambda: finish("P", (1,))), ("send-1", lambda: finish("P", (-1,)))]
    ready2 = lambda o: finish("P", (o,)) and now >= sent.get("send-3", 1e9) + 4.5
    after += [("send2", lambda: ready2(2) and ready2(-2))]
    sent = {}
    while todo or events or after:
        while events and events[0][1] <= now:
            out.append((events.pop(0)[0],))
            now += 0.05
        for item in list(after):
            if item[1]():
                out.append((item[0],))
                sent[item[0]] = now
                after.remove(item)
                if item[0] == "total":
                    events.append(("plane", now + 7.0))
        pick = None
        for task in todo:
            kind, o, g = task
            if kind == "S":
                if max(GROUP_AT[g], ROW_AT[o]) <= now:
                    pick = task
                    break
            elif ("S", o, g) in done:
                pick = task
                break
        if pick is None:
            now += 0.05
            continue
        todo.remove(pick)
        done.add(pick)
        out.append(pick)
        core, a, b = GROUPS[pick[2]]
        now += (b - a) * (SCORE_US if pick[0] == "S" else PULL_US)
    return out


def dot(a, b):
    return lax.dot_general(a, b, (((1,), (0,)), ((), ())), preferred_element_type=F32)


def encode(x, msg, cols):
    top = (jnp.max(jnp.abs(x), axis=0, keepdims=True) * 1.01 + 1e-30).astype(BF16)
    y = jnp.exp2(jnp.abs(x) * (SPAN / top.astype(F32)) - SPAN / 2)
    msg[0:D, cols] = jnp.where(x < 0, -y, y).astype(BF16)
    msg[D:MSG, cols] = jnp.broadcast_to(top, (MSG - D, x.shape[1]))


def decode(msg, cols):
    y = msg[0:D, cols].astype(F32)
    top = msg[D:MSG, cols].astype(F32)[0:1]
    x = (jnp.log(jnp.abs(y)) * (1.0 / math.log(2.0)) + SPAN / 2) * (top * (1.0 / SPAN))
    return jnp.where(y < 0, -x, x)


class Net:
    def __init__(self, send, recv):
        t, m = lax.axis_index("tour"), lax.axis_index("team")
        self.z = (t // 4) * 2 + (m // 2) % 2
        self.x, self.y, self.c = t % 4, m // 4, m % 2
        self.send, self.recv, self.groups, self.known = send, recv, [], {}

    def step(self, axis, d, n):
        if (axis, d) not in self.known:
            v = getattr(self, axis) + d
            v = jnp.where(v >= n, v - n, v) if d else v
            self.known[axis, d] = (v // 2, v % 2) if axis == "z" else v
        return self.known[axis, d]

    def at(self, dx=0, dy=0, dz=0, dc=0):
        z = self.step("z", dz % NZ, NZ)
        return (z[0] * 4 + self.step("x", dx % NX, NX),
                self.step("y", dy % NY, NY) * 4 + z[1] * 2 + self.step("c", dc, 2))


class Group:
    def __init__(self, net, size, *copies):
        i = len(net.groups)
        net.groups.append(self)
        sems = dict(send_sem=net.send.at[i], recv_sem=net.recv.at[i], device_id_type=MESH)
        self.copies = [
            pltpu.make_async_remote_copy(src_ref=a, dst_ref=b, device_id=net.at(**where), **sems) for a, b, where in copies]
        self.all = pltpu.make_async_remote_copy(src_ref=size, dst_ref=size, device_id=net.at(dc=1), **sems)

    def start(self):
        for c in self.copies:
            c.start()

    def wait_recv(self):
        self.all.wait_recv()

    def wait_send(self):
        self.all.wait_send()


NUM_GROUPS = 4 + 5 + 6 + 6 + 2


def kernel(emb_ref, out_ref, tot_ref, cols, colt, rowt, acc, w, once, twice, mo, mi, sums, send, recv):
    net = Net(send, recv)
    line = [(dz, dc) for dz in range(NZ) for dc in range(2) if (dz, dc) != (0, 0)]
    plane = [(dx, dy) for dx in range(NX) for dy in range(NY) if (dx, dy) != (0, 0)]

    barrier = pltpu.get_barrier_semaphore()
    for dz, dc in line:
        pl.semaphore_signal(barrier, inc=1, device_id=net.at(dz=dz, dc=dc), device_id_type=MESH)
    for dx, dy in plane:
        pl.semaphore_signal(barrier, inc=1, device_id=net.at(dx=dx, dy=dy), device_id_type=MESH)

    row = lambda o: rowt.at[SLOT[o]]
    rows1 = Group(net, rowt.at[1:3], (row(0), row(-1), dict(dz=1)), (row(0), row(1), dict(dz=-1)))
    rows2 = Group(net, rowt.at[3:5], (row(-1), row(-2), dict(dz=1)), (row(1), row(2), dict(dz=-1)))
    rows3 = Group(net, rowt.at[5:7], (row(-1), row(-3), dict(dz=2)), (row(1), row(3), dict(dz=-2)))
    rows4 = Group(net, row(4), (row(0), row(4), dict(dz=4)))
    place = lambda dx, dy: PLACE[dx % NX, dy % NY]
    along = lambda dx, dy: (cols.at[0, 0], cols.at[0, place(-dx, -dy)], dict(dx=dx, dy=dy))
    by_y = lambda a, b, s: (cols.at[0, place(a, 0), s], cols.at[0, place(a, -b), s], dict(dy=b))
    by_x = lambda a, b, s: (cols.at[0, place(0, a), s], cols.at[0, place(-b, a), s], dict(dx=b))
    cols1 = Group(net, cols.at[0, 1:5], along(1, 0), along(3, 0), along(0, 1), along(0, 3))
    cols2 = Group(net, cols.at[0, 5:7], along(2, 0), along(0, 2))
    cols3 = Group(net, cols.at[0, 7:11], *[f(a, b, s) for b in (1, 3) for a in (1, 3) for f, s in ((by_y, LO), (by_x, HI))])
    cols4 = Group(net, cols.at[0, 11:15], *[f(a, 2, ALL) for a in (1, 3) for f in (by_y, by_x)])
    cols5 = Group(net, cols.at[0, 15], by_y(2, 2, LO), by_x(2, 2, HI))
    sib = [Group(net, cols.at[1, a:b], (cols.at[0, a:b], cols.at[1, a:b], dict(dc=1)))
           for a, b in ((0, 1), (1, 5), (5, 7), (7, 11), (11, 15), (15, 16))]
    msg = lambda o: mo.at[SLOT[o]]
    far = Group(net, mi.at[0], (msg(4).at[:, LO], mi.at[0, :, LO], dict(dz=2)), (msg(4).at[:, HI], mi.at[0, :, HI], dict(dz=-2)))
    third = {3: Group(net, mi.at[1], (msg(3), mi.at[1], dict(dz=1))), -3: Group(net, mi.at[2], (msg(-3), mi.at[2], dict(dz=-1)))}
    second = Group(net, mi.at[3:5], (msg(2), mi.at[3], dict(dz=2)), (msg(-2), mi.at[4], dict(dz=-2)))
    first = {1: Group(net, mi.at[5], (msg(1), mi.at[5], dict(dz=1))), -1: Group(net, mi.at[6], (msg(-1), mi.at[6], dict(dz=-1)))}
    tell_line = Group(net, sums.at[1:16], *[(sums.at[0], sums.at[1 + i], dict(dz=dz, dc=dc)) for i, (dz, dc) in enumerate(line)])
    tell_plane = Group(
        net, sums.at[17:32], *[(sums.at[16], sums.at[17 + i], dict(dx=dx, dy=dy)) for i, (dx, dy) in enumerate(plane)])

    emb = emb_ref[...]
    inv_norm = lax.rsqrt(jnp.sum(emb * emb, axis=1, keepdims=True) + 1e-06)
    direction = emb * inv_norm
    own = direction.astype(BF16)
    wide = own.astype(F32)
    cols[0, 0] = own
    rowt[0] = wide.T.astype(BF16)
    self_weight = jnp.exp(4.0 * jnp.sum(wide * wide, axis=1, keepdims=True) - 4.0)
    once[...] = jnp.zeros_like(once)
    twice[...] = jnp.zeros_like(twice)
    pl.semaphore_wait(barrier, len(line) + len(plane))

    for c in (rows1, cols1, cols2, rows4, sib[0]):
        c.start()

    turned, begun = set(), set()

    def scores(o, g):
        core, a, b = GROUPS[g]
        n = (b - a) * B
        r = (core * 16 + a) * B
        e = jnp.exp2(dot(cols[core, a:b].reshape(n, D), rowt[SLOT[o]]) * SCALE)
        if o >= 0:
            total = once if o in (0, 4) else twice
            total[...] += jnp.sum(e.reshape(n // 64, 64, B), axis=0)
        w[SLOT[o], r:r + n] = e.astype(BF16)

    def pull(o, g):
        core, a, b = GROUPS[g]
        n = (b - a) * B
        r = (core * 16 + a) * B
        if g not in turned:
            turned.add(g)
            for k in range(a, b):
                s = (core * 16 + k) * B
                colt[:, s:s + B] = cols[core, k].astype(F32).T.astype(BF16)
        p = dot(colt[:, r:r + n], w[SLOT[o], r:r + n])
        if o in begun:
            acc[SLOT[o]] += p
        else:
            begun.add(o)
            acc[SLOT[o]] = p

    def event(name):
        if name == "rows1":
            rows1.wait_recv()
            rows2.start()
            rows3.start()
        elif name.startswith("rows"):
            {"rows2": rows2, "rows3": rows3, "rows4": rows4}[name].wait_recv()
        elif name.startswith("cols"):
            k = int(name[4:])
            (cols1, cols2, cols3, cols4, cols5)[k - 1].wait_recv()
            sib[k].start()
            if k == 1:
                cols3.start()
                cols4.start()
            if k == 2:
                cols5.start()
        elif name.startswith("sib"):
            sib[int(name[3:])].wait_recv()
            if name == "sib1":
                sib[0].wait_recv()
        elif name == "total":
            local = (2.0 * jnp.sum(twice[...]) + jnp.sum(once[...])) * SHIFT - jnp.sum(self_weight)
            sums[0] = jnp.full((8, 128), local, F32)
            tell_line.start()
        elif name == "plane":
            tell_line.wait_recv()
            total = sums[0]
            for i in range(len(line)):
                total = total + sums[1 + i]
            sums[16] = total
            tell_plane.start()
        elif name == "send2":
            far.wait_recv()
            for o, half, i in ((2, LO, 1), (-2, HI, 2)):
                third[3 if o > 0 else -3].wait_recv()
                p = SLOT[o]
                acc[p, :, half] += decode(mi.at[0], half)
                encode(acc[p] + decode(mi.at[i], ALL), mo.at[p], ALL)
            second.start()
        else:
            o = int(name[4:])
            encode(acc[SLOT[o]], mo.at[SLOT[o]], ALL)
            {4: far, 3: third[3], -3: third[-3], 1: first[1], -1: first[-1]}[o].start()

    for task in plan():
        if task[0] == "S":
            scores(*task[1:])
        elif task[0] == "P":
            pull(*task[1:])
        else:
            event(task[0])

    pulled = acc[0]
    for c, held in ((first[-1], (6,)), (first[1], (5,)), (second, (3, 4))):
        c.wait_recv()
        for i in held:
            pulled = pulled + decode(mi.at[i], ALL)
    pulled = pulled.T * SHIFT - self_weight * wide
    radial = jnp.sum(direction * pulled, axis=1, keepdims=True)
    out_ref[...] = inv_norm * (pulled - direction * radial)
    tell_plane.wait_recv()
    total = sums[16]
    for i in range(len(plane)):
        total = total + sums[17 + i]
    tot_ref[...] = total
    for c in net.groups:
        c.wait_send()


def per_device(embeddings):
    whole = pl.BlockSpec(memory_space=pltpu.VMEM)
    raw, total = pl.pallas_call(
        kernel,
        out_shape=(jax.ShapeDtypeStruct((B, D), F32), jax.ShapeDtypeStruct((8, 128), F32)),
        in_specs=[whole],
        out_specs=(whole, whole),
        scratch_shapes=[
            pltpu.VMEM((2, 16, B, D), BF16),
            pltpu.VMEM((D, 32 * B), BF16),
            pltpu.VMEM((8, D, B), BF16),
            pltpu.VMEM((8, D, B), F32),
            pltpu.VMEM((8, 32 * B, B), BF16),
            pltpu.VMEM((64, B), F32),
            pltpu.VMEM((64, B), F32),
            pltpu.VMEM((8, MSG, B), BF16),
            pltpu.VMEM((8, MSG, B), BF16),
            pltpu.VMEM((32, 8, 128), F32),
            pltpu.SemaphoreType.DMA((NUM_GROUPS,)),
            pltpu.SemaphoreType.DMA((NUM_GROUPS,)),
        ],
        compiler_params=pltpu.CompilerParams(
            collective_id=0, has_side_effects=True, vmem_limit_bytes=56 * 2**20),
        name="uniformity",
    )(embeddings)
    pair_total = total[0, 0]
    rows = float(B * lax.axis_size("tour") * lax.axis_size("team"))
    loss = jnp.log(pair_total / (rows * (rows - 1.0)))
    return raw * (rows * rows / 8.0 / pair_total), loss


def solution(mesh):
    return jax.shard_map(
        per_device,
        mesh=mesh,
        in_specs=(P(("tour", "team"), None),),
        out_specs=(P(("tour", "team"), None), P()),
        check_vma=False,
    )
```

time: 50.9 us -> 50.5 us (level)
  no operation moved by 1% of the time
where the time goes in v2:
time: 50.5 us; the launch traced here: 50.4 us
  Pallas kernels  44.5 us (88%)
  between operations  3.14 us (6%)
  other arithmetic  1.57 us (3%)
  local copies, waits for them, and re-layouts  1.2 us (2%)
    pallas_call x1, Pallas kernels, per_device(): pl.pallas_call(kernel, out_shape=(jax.ShapeDtypeStruct((B, D), F32), jax....  44.5 us
    mul x1, other arithmetic, per_device(): return (raw * (rows * rows / 8.0 / pair_total), loss)  1.57 us
    slice x1, local copies, waits for them, and re-layouts, per_device(): pair_total = total[0, 0]  1.2 us

profile of v2, /device:TPU:1, one launch (start us, length us, event | category | flops | bytes accessed | tf_op | source)
XLA Modules:
  0.0 50.4 jit_solution(66360566369427364)
XLA Ops:
  0.6 44.5 %uniformity.1 = (f32[256,128]{1,0:T(8,128)}, f32[8,128]{1,0:T(8,128)}) custom-call(f32[256,128]{1,0:T(8,128)} %emb_ref.1), custom_call_target="tpu_custom_call" | custom-call | tf_op jit(solution)/shard_map/uniformity/pallas_call | solution.py:304
  45.1 1.2 %slice.3 = f32[1,1]{1,0:T(1,128)} slice(f32[8,128]{1,0:T(8,128)} %get-tuple-element.5), slice={[0:1], [0:1]} | slice | bytes 8 | tf_op jit(solution)/shard_map/slice | solution.py:327
  47.7 1.6 %broadcast_multiply_fusion = f32[256,128]{1,0:T(8,128)} fusion(f32[256,128]{1,0:T(8,128)} %get-tuple-element.4, f32[]{:T(128)} %bitcast), kind=kLoop, calls=%fused_computation | loop fusion | flops 32768 | bytes 262148 | tf_op jit(solution)/shard_map/mul | solution.py:330

commit v3 on v2

--- a/solution.py
+++ b/solution.py
@@ -25,8 +25,8 @@
 PLACE = {chip: k for k, chip in enumerate(CHIPS)}
 GROUPS = ((0, 0, 5), (1, 0, 5), (0, 5, 7), (1, 5, 7), (0, 7, 11), (1, 7, 11), (0, 11, 15), (1, 11, 15), (0, 15, 16),
           (1, 15, 16))
-EVENTS = (("rows1", 3.1), ("cols1", 3.2), ("sib1", 4.9), ("cols2", 5.4), ("sib2", 6.9), ("rows2", 7.5), ("cols3", 7.6),
-          ("rows4", 8.4), ("sib3", 9.1), ("cols4", 9.2), ("cols5", 10.2), ("rows3", 10.5), ("sib4", 10.8), ("sib5", 11.7))
+EVENTS = (("rows1", 3.1), ("cols1", 3.1), ("cols2", 5.2), ("sib1", 5.2), ("rows2", 7.4), ("cols3", 7.4), ("sib2", 7.4),
+          ("rows4", 8.9), ("sib3", 8.9), ("cols4", 10.0), ("cols5", 10.0), ("rows3", 10.4), ("sib4", 11.5), ("sib5", 11.5))
 AT = dict(EVENTS)
 GROUP_AT = tuple(AT[e] for e in ("cols1", "sib1", "cols2", "sib2", "cols3", "sib3", "cols4", "sib4",
                                 "cols5", "sib5"))
@@ -38,9 +38,8 @@
 def plan():
     events = list(EVENTS)
     n = len(GROUPS)
-    goals = [("S", o, g) for g in range(n) for o in (0, 1, 2, 3, 4)]
-    goals += [("S", -3, g) for g in range(n)]
-    goals += [("P", o, g) for o in (4, 3, -3) for g in range(n)]
+    goals = [(kind, o, g) for o in (4, 3, -3) for kind in "SP" for g in range(n)]
+    goals += [("S", o, g) for g in range(n) for o in (0, 1, 2)]
     for o in (2, 1):
         goals += [("S", -o, g) for g in range(n)]
         goals += [("P", s * o, g) for s in (-1, 1) for g in range(n)]
@@ -55,7 +54,7 @@
     after += [("send4", lambda: finish("P", (4,)))]
     after += [("send3", lambda: finish("P", (3,))), ("send-3", lambda: finish("P", (-3,)))]
     after += [("send1", lambda: finish("P", (1,))), ("send-1", lambda: finish("P", (-1,)))]
-    ready2 = lambda o: finish("P", (o,)) and now >= sent.get("send-3", 1e9) + 4.5
+    ready2 = lambda o: finish("P", (o,)) and now >= sent.get("send-3", 1e9) + 4.2
     after += [("send2", lambda: ready2(2) and ready2(-2))]
     sent = {}
     while todo or events or after:
@@ -68,7 +67,7 @@
                 sent[item[0]] = now
                 after.remove(item)
                 if item[0] == "total":
-                    events.append(("plane", now + 7.0))
+                    events.append(("plane", now + 5.5))
         pick = None
         for task in todo:
             kind, o, g = task
@@ -151,7 +150,7 @@
 NUM_GROUPS = 4 + 5 + 6 + 6 + 2
 
 
-def kernel(emb_ref, out_ref, tot_ref, cols, colt, rowt, acc, w, once, twice, mo, mi, sums, send, recv):
+def kernel(emb_hbm, out_ref, loss_ref, emb_ref, fetched, cols, colt, rowt, acc, w, once, twice, mo, mi, sums, send, recv):
     net = Net(send, recv)
     line = [(dz, dc) for dz in range(NZ) for dc in range(2) if (dz, dc) != (0, 0)]
     plane = [(dx, dy) for dx in range(NX) for dy in range(NY) if (dx, dy) != (0, 0)]
@@ -161,6 +160,9 @@
         pl.semaphore_signal(barrier, inc=1, device_id=net.at(dz=dz, dc=dc), device_id_type=MESH)
     for dx, dy in plane:
         pl.semaphore_signal(barrier, inc=1, device_id=net.at(dx=dx, dy=dy), device_id_type=MESH)
+
+    fetch = pltpu.make_async_copy(emb_hbm, emb_ref, fetched)
+    fetch.start()
 
     row = lambda o: rowt.at[SLOT[o]]
     rows1 = Group(net, rowt.at[1:3], (row(0), row(-1), dict(dz=1)), (row(0), row(1), dict(dz=-1)))
@@ -187,6 +189,7 @@
     tell_plane = Group(
         net, sums.at[17:32], *[(sums.at[16], sums.at[17 + i], dict(dx=dx, dy=dy)) for i, (dx, dy) in enumerate(plane)])
 
+    fetch.wait()
     emb = emb_ref[...]
     inv_norm = lax.rsqrt(jnp.sum(emb * emb, axis=1, keepdims=True) + 1e-06)
     direction = emb * inv_norm
@@ -289,24 +292,28 @@
             pulled = pulled + decode(mi.at[i], ALL)
     pulled = pulled.T * SHIFT - self_weight * wide
     radial = jnp.sum(direction * pulled, axis=1, keepdims=True)
-    out_ref[...] = inv_norm * (pulled - direction * radial)
+    grad = inv_norm * (pulled - direction * radial)
     tell_plane.wait_recv()
     total = sums[16]
     for i in range(len(plane)):
         total = total + sums[17 + i]
-    tot_ref[...] = total
+    rows = float(B * lax.axis_size("tour") * lax.axis_size("team"))
+    out_ref[...] = grad * jnp.broadcast_to((rows * rows / 8.0) / total[0:1], (B, D))
+    loss_ref[0, 0] = jnp.max(jnp.log(total / (rows * (rows - 1.0))))
     for c in net.groups:
         c.wait_send()
 
 
 def per_device(embeddings):
     whole = pl.BlockSpec(memory_space=pltpu.VMEM)
-    raw, total = pl.pallas_call(
+    grad, loss = pl.pallas_call(
         kernel,
-        out_shape=(jax.ShapeDtypeStruct((B, D), F32), jax.ShapeDtypeStruct((8, 128), F32)),
-        in_specs=[whole],
-        out_specs=(whole, whole),
+        out_shape=(jax.ShapeDtypeStruct((B, D), F32), jax.ShapeDtypeStruct((1, 1), F32)),
+        in_specs=[pl.BlockSpec(memory_space=pltpu.HBM)],
+        out_specs=(whole, pl.BlockSpec(memory_space=pltpu.SMEM)),
         scratch_shapes=[
+            pltpu.VMEM((B, D), F32),
+            pltpu.SemaphoreType.DMA,
             pltpu.VMEM((2, 16, B, D), BF16),
             pltpu.VMEM((D, 32 * B), BF16),
             pltpu.VMEM((8, D, B), BF16),
@@ -324,10 +331,7 @@
             collective_id=0, has_side_effects=True, vmem_limit_bytes=56 * 2**20),
         name="uniformity",
     )(embeddings)
-    pair_total = total[0, 0]
-    rows = float(B * lax.axis_size("tour") * lax.axis_size("team"))
-    loss = jnp.log(pair_total / (rows * (rows - 1.0)))
-    return raw * (rows * rows / 8.0 / pair_total), loss
+    return grad, loss.reshape(())
 
 
 def solution(mesh):

time: 50.5 us -> 48.3 us (0.956)
  other arithmetic: 1.57 us -> 0 us
  between operations: 3.14 us -> 2.45 us
    mul x1 -> x0, other arithmetic: 1.57 us -> none  [per_device(): return (raw * (rows * rows / 8.0 / pair_total), loss)]
    unnamed x0 -> x1, local copies, waits for them, and re-layouts: none -> 1.57 us
    slice x1 -> x0, local copies, waits for them, and re-layouts: 1.2 us -> none  [per_device(): pair_total = total[0, 0]]
where the time goes in v3:
time: 48.3 us; the launch traced here: 48.1 us
  Pallas kernels  44.1 us (91%)
  between operations  2.45 us (5%)
  local copies, waits for them, and re-layouts  1.57 us (3%)
    pallas_call x1, Pallas kernels, per_device(): pl.pallas_call(kernel, out_shape=(jax.ShapeDtypeStruct((B, D), F32), jax....  44.1 us
    unnamed x1, local copies, waits for them, and re-layouts  1.57 us

profile of v3, /device:TPU:1, one launch (start us, length us, event | category | flops | bytes accessed | tf_op | source)
XLA Modules:
  0.0 48.1 jit_solution(9419952325594145123)
XLA Ops:
  0.6 44.1 %uniformity.1 = (f32[256,128]{1,0:T(8,128)}, f32[1,1]{1,0:T(1,128)}) custom-call(f32[256,128]{1,0:T(8,128)} %emb_hbm.1), custom_call_target="tpu_custom_call" | custom-call | tf_op jit(solution)/shard_map/uniformity/pallas_call | solution.py:309
  44.8 1.6 %copy.5 = f32[256,128]{1,0:T(8,128)} copy(f32[256,128]{1,0:T(8,128)} %get-tuple-element.8) | data formatting | bytes 262144

commit v4 on v3

--- a/solution.py
+++ b/solution.py
@@ -67,7 +67,7 @@
                 sent[item[0]] = now
                 after.remove(item)
                 if item[0] == "total":
-                    events.append(("plane", now + 5.5))
+                    events += [("told1", now + 4.2), ("told2", now + 7.4)]
         pick = None
         for task in todo:
             kind, o, g = task
@@ -147,20 +147,19 @@
         self.all.wait_send()
 
 
-NUM_GROUPS = 4 + 5 + 6 + 6 + 2
-
-
-def kernel(emb_hbm, out_ref, loss_ref, emb_ref, fetched, cols, colt, rowt, acc, w, once, twice, mo, mi, sums, send, recv):
+NUM_GROUPS = 4 + 5 + 6 + 6 + 3
+
+
+def kernel(emb_hbm, out_ref, loss_ref, factor_ref, emb_ref, fetched, cols, colt, rowt, acc, w, once, twice, mo, mi, sums, send, recv):
     net = Net(send, recv)
-    line = [(dz, dc) for dz in range(NZ) for dc in range(2) if (dz, dc) != (0, 0)]
-    plane = [(dx, dy) for dx in range(NX) for dy in range(NY) if (dx, dy) != (0, 0)]
+    along_z = [dict(dz=d) for d in range(1, NZ)]
+    along_x = [dict(dx=d, dc=c) for d in range(NX) for c in range(2) if (d, c) != (0, 0)]
+    along_y = [dict(dy=d) for d in range(1, NY)]
+    met = along_z + along_x + along_y
 
     barrier = pltpu.get_barrier_semaphore()
-    for dz, dc in line:
-        pl.semaphore_signal(barrier, inc=1, device_id=net.at(dz=dz, dc=dc), device_id_type=MESH)
-    for dx, dy in plane:
-        pl.semaphore_signal(barrier, inc=1, device_id=net.at(dx=dx, dy=dy), device_id_type=MESH)
-
+    for where in met:
+        pl.semaphore_signal(barrier, inc=1, device_id=net.at(**where), device_id_type=MESH)
     fetch = pltpu.make_async_copy(emb_hbm, emb_ref, fetched)
     fetch.start()
 
@@ -185,9 +184,17 @@
     third = {3: Group(net, mi.at[1], (msg(3), mi.at[1], dict(dz=1))), -3: Group(net, mi.at[2], (msg(-3), mi.at[2], dict(dz=-1)))}
     second = Group(net, mi.at[3:5], (msg(2), mi.at[3], dict(dz=2)), (msg(-2), mi.at[4], dict(dz=-2)))
     first = {1: Group(net, mi.at[5], (msg(1), mi.at[5], dict(dz=1))), -1: Group(net, mi.at[6], (msg(-1), mi.at[6], dict(dz=-1)))}
-    tell_line = Group(net, sums.at[1:16], *[(sums.at[0], sums.at[1 + i], dict(dz=dz, dc=dc)) for i, (dz, dc) in enumerate(line)])
-    tell_plane = Group(
-        net, sums.at[17:32], *[(sums.at[16], sums.at[17 + i], dict(dx=dx, dy=dy)) for i, (dx, dy) in enumerate(plane)])
+    tell = []
+    for base, peers in ((0, along_z), (8, along_x), (16, along_y)):
+        tell.append(Group(net, sums.at[base + 1:base + 1 + len(peers)],
+                          *[(sums.at[base], sums.at[base + 1 + i], where) for i, where in enumerate(peers)]))
+
+    def told(r):
+        tell[r].wait_recv()
+        total = sums[8 * r]
+        for i in range(len(tell[r].copies)):
+            total = total + sums[8 * r + 1 + i]
+        return total
 
     fetch.wait()
     emb = emb_ref[...]
@@ -200,7 +207,7 @@
     self_weight = jnp.exp(4.0 * jnp.sum(wide * wide, axis=1, keepdims=True) - 4.0)
     once[...] = jnp.zeros_like(once)
     twice[...] = jnp.zeros_like(twice)
-    pl.semaphore_wait(barrier, len(line) + len(plane))
+    pl.semaphore_wait(barrier, len(met))
 
     for c in (rows1, cols1, cols2, rows4, sib[0]):
         c.start()
@@ -256,14 +263,11 @@
         elif name == "total":
             local = (2.0 * jnp.sum(twice[...]) + jnp.sum(once[...])) * SHIFT - jnp.sum(self_weight)
             sums[0] = jnp.full((8, 128), local, F32)
-            tell_line.start()
-        elif name == "plane":
-            tell_line.wait_recv()
-            total = sums[0]
-            for i in range(len(line)):
-                total = total + sums[1 + i]
-            sums[16] = total
-            tell_plane.start()
+            tell[0].start()
+        elif name.startswith("told"):
+            r = int(name[4:])
+            sums[8 * r] = told(r - 1)
+            tell[r].start()
         elif name == "send2":
             far.wait_recv()
             for o, half, i in ((2, LO, 1), (-2, HI, 2)):
@@ -292,25 +296,22 @@
             pulled = pulled + decode(mi.at[i], ALL)
     pulled = pulled.T * SHIFT - self_weight * wide
     radial = jnp.sum(direction * pulled, axis=1, keepdims=True)
-    grad = inv_norm * (pulled - direction * radial)
-    tell_plane.wait_recv()
-    total = sums[16]
-    for i in range(len(plane)):
-        total = total + sums[17 + i]
+    out_ref[...] = inv_norm * (pulled - direction * radial)
+    total = told(2)
     rows = float(B * lax.axis_size("tour") * lax.axis_size("team"))
-    out_ref[...] = grad * jnp.broadcast_to((rows * rows / 8.0) / total[0:1], (B, D))
     loss_ref[0, 0] = jnp.max(jnp.log(total / (rows * (rows - 1.0))))
+    factor_ref[0, 0] = jnp.max((rows * rows / 8.0) / total)
     for c in net.groups:
         c.wait_send()
 
 
 def per_device(embeddings):
     whole = pl.BlockSpec(memory_space=pltpu.VMEM)
-    grad, loss = pl.pallas_call(
+    grad, loss, factor = pl.pallas_call(
         kernel,
-        out_shape=(jax.ShapeDtypeStruct((B, D), F32), jax.ShapeDtypeStruct((1, 1), F32)),
+        out_shape=(jax.ShapeDtypeStruct((B, D), F32), jax.ShapeDtypeStruct((1, 1), F32), jax.ShapeDtypeStruct((1, 1), F32)),
         in_specs=[pl.BlockSpec(memory_space=pltpu.HBM)],
-        out_specs=(whole, pl.BlockSpec(memory_space=pltpu.SMEM)),
+        out_specs=(whole, pl.BlockSpec(memory_space=pltpu.SMEM), pl.BlockSpec(memory_space=pltpu.SMEM)),
         scratch_shapes=[
             pltpu.VMEM((B, D), F32),
             pltpu.SemaphoreType.DMA,
@@ -323,7 +324,7 @@
             pltpu.VMEM((64, B), F32),
             pltpu.VMEM((8, MSG, B), BF16),
             pltpu.VMEM((8, MSG, B), BF16),
-            pltpu.VMEM((32, 8, 128), F32),
+            pltpu.VMEM((20, 8, 128), F32),
             pltpu.SemaphoreType.DMA((NUM_GROUPS,)),
             pltpu.SemaphoreType.DMA((NUM_GROUPS,)),
         ],
@@ -331,7 +332,7 @@
             collective_id=0, has_side_effects=True, vmem_limit_bytes=56 * 2**20),
         name="uniformity",
     )(embeddings)
-    return grad, loss.reshape(())
+    return grad * factor.reshape(()), loss.reshape(())
 
 
 def solution(mesh):

time: 48.3 us -> 49.8 us (1.031)
  other arithmetic: 0 us -> 2.19 us
  local copies, waits for them, and re-layouts: 1.57 us -> 0 us
  Pallas kernels: 44.1 us -> 45 us
    mul x0 -> x1, other arithmetic: none -> 2.19 us  [per_device(): return (grad * factor.reshape(()), loss.reshape(()))]
    unnamed x1 -> x0, local copies, waits for them, and re-layouts: 1.57 us -> none
    pallas_call x1, Pallas kernels: 44.1 us -> 45 us  [per_device(): pl.pallas_call(kernel, out_shape=(jax.ShapeDtypeStruct((B, D), F32), jax....]
where the time goes in v4:
time: 49.8 us; the launch traced here: 49.7 us
  Pallas kernels  45 us (90%)
  between operations  2.45 us (5%)
  other arithmetic  2.19 us (4%)
    pallas_call x1, Pallas kernels, per_device(): pl.pallas_call(kernel, out_shape=(jax.ShapeDtypeStruct((B, D), F32), jax....  45 us
    mul x1, other arithmetic, per_device(): return (grad * factor.reshape(()), loss.reshape(()))  2.19 us

profile of v4, /device:TPU:1, one launch (start us, length us, event | category | flops | bytes accessed | tf_op | source)
XLA Modules:
  0.0 49.7 jit_solution(5389752544886660613)
XLA Ops:
  0.6 45.0 %uniformity.1 = (f32[256,128]{1,0:T(8,128)}, f32[1,1]{1,0:T(1,128)}, f32[1,1]{1,0:T(1,128)}) custom-call(f32[256,128]{1,0:T(8,128)} %emb_hbm.1), custom_call_target="tpu_custom_call" | custom-call | tf_op jit(solution)/shard_map/uniformity/pallas_call | solution.py:310
  45.7 2.2 %broadcast_multiply_fusion = f32[256,128]{1,0:T(8,128)} fusion(f32[256,128]{1,0:T(8,128)} %get-tuple-element.5, f32[]{:T(128)} %bitcast), kind=kLoop, calls=%fused_computation | loop fusion | flops 32768 | bytes 262148 | tf_op jit(solution)/shard_map/mul | solution.py:335

commit v5 on v3

--- a/solution.py
+++ b/solution.py
@@ -54,7 +54,7 @@
     after += [("send4", lambda: finish("P", (4,)))]
     after += [("send3", lambda: finish("P", (3,))), ("send-3", lambda: finish("P", (-3,)))]
     after += [("send1", lambda: finish("P", (1,))), ("send-1", lambda: finish("P", (-1,)))]
-    ready2 = lambda o: finish("P", (o,)) and now >= sent.get("send-3", 1e9) + 4.2
+    ready2 = lambda o: finish("P", (o,)) and now >= sent.get("send-3", 1e9) + 3.2
     after += [("send2", lambda: ready2(2) and ready2(-2))]
     sent = {}
     while todo or events or after:
@@ -308,7 +308,7 @@
     whole = pl.BlockSpec(memory_space=pltpu.VMEM)
     grad, loss = pl.pallas_call(
         kernel,
-        out_shape=(jax.ShapeDtypeStruct((B, D), F32), jax.ShapeDtypeStruct((1, 1), F32)),
+        out_shape=(pltpu.VMEM((B, D), F32), jax.ShapeDtypeStruct((1, 1), F32)),
         in_specs=[pl.BlockSpec(memory_space=pltpu.HBM)],
         out_specs=(whole, pl.BlockSpec(memory_space=pltpu.SMEM)),
         scratch_shapes=[

time: 48.3 us -> 46.7 us (0.967)
  local copies, waits for them, and re-layouts: 1.57 us -> 0.66 us
  Pallas kernels: 44.1 us -> 43.6 us
    unnamed x1, local copies, waits for them, and re-layouts: 1.57 us -> 0.66 us
    pallas_call x1, Pallas kernels: 44.1 us -> 43.6 us  [per_device(): pl.pallas_call(kernel, out_shape=(pltpu.VMEM((B, D), F32), jax.ShapeDtype...]
where the time goes in v5:
time: 46.7 us; the launch traced here: 46.6 us
  Pallas kernels  43.6 us (93%)
  between operations  2.33 us (5%)
  local copies, waits for them, and re-layouts  0.66 us (1%)
    pallas_call x1, Pallas kernels, per_device(): pl.pallas_call(kernel, out_shape=(pltpu.VMEM((B, D), F32), jax.ShapeDtype...  43.6 us

profile of v5, /device:TPU:1, one launch (start us, length us, event | category | flops | bytes accessed | tf_op | source)
XLA Modules:
  0.0 46.6 jit_solution(12454958474309824277)
XLA Ops:
  0.6 43.6 %uniformity.1 = (f32[256,128]{1,0:T(8,128)S(1)}, f32[1,1]{1,0:T(1,128)}) custom-call(f32[256,128]{1,0:T(8,128)} %emb_hbm.1), custom_call_target="tpu_custom_call" | custom-call | tf_op jit(solution)/shard_map/uniformity/pallas_call | solution.py:309
  44.3 0.7 %copy.5 = f32[256,128]{1,0:T(8,128)} copy(f32[256,128]{1,0:T(8,128)S(1)} %get-tuple-element.6) | data formatting | bytes 262144
